TPU v7x, 256 devices: a whole 4x4x8 slice. The times are simulated.
256 devices in a mesh: ax: 32 (over y, z_lo, core), ay: 4 (over x), fr: 2 (over z_hi).
Axes of the slice: x: 4, y: 4, z: 8 (z_hi: 2, z_lo: 4; z = z_hi * 4 + z_lo), core: 2. Of those that a mesh axis runs over, the one named last changes fastest.
Arguments:
- echoes: float32 [128, 2, 1024, 512], P('fr', None, 'ax', 'ay'), may hold values from -6 to 6
- stolt_table: float32 [8, 128, 128], replicated, may hold values from -0.5 to 0.5
- kz_start: int32 [1024, 4], P(('ay', 'ax', 'fr')), may hold values from 0 to 1
- weight_ids: int32 [1024, 4, 2], P(('ay', 'ax', 'fr')), may hold values from 0 to 7
Outputs:
- image: float32 [2, 1024, 512, 384], P(None, ('ay', 'ax', 'fr'))
All inputs are finite; a program needn't handle non-finite values.
Results may differ from a plain program's by a relative error of at most 0.0003.
Values sent between devices are 32-bit elements; how exact they have to be, the bound alone decides.
No kernel may reach another device: no remote copies, remote signals or barrier semaphores. Data moves between devices by JAX's collectives and lax.ppermute only.
A program may use at most 128 MiB of HBM per device.

v0:
```python
import functools
import math

import jax
import jax.numpy as jnp
import ml_dtypes
import numpy as np
from jax import lax
from jax.experimental import pallas as pl
from jax.experimental.pallas import tpu as pltpu
from jax.sharding import PartitionSpec as P

TK = 128
KZ = 384
LANES = 128


def halves_of(table):
    high = table.astype(ml_dtypes.bfloat16)
    low = (table - high.astype(np.float64)).astype(ml_dtypes.bfloat16)
    return np.stack([high, low])


def radix4_tables(length):
    quarter = length // 4
    n = np.arange(quarter)
    tables = []
    for r in range(4):
        phase = ((4 * np.arange(quarter)[:, None] + r) * n[None, :]) % length
        angle = phase * (2.0 * math.pi / length)
        cosine, sine = np.cos(angle) / math.sqrt(length), np.sin(angle) / math.sqrt(length)
        tables.append(halves_of(np.block([[cosine, sine], [-sine, cosine]])))
    return np.stack(tables)


def inverse_table(length):
    index = np.arange(length)
    angle = (index[:, None] * index[None, :] % length) * (2.0 * math.pi / length)
    return halves_of(np.concatenate([np.cos(angle), np.sin(angle)], axis=1) / math.sqrt(length))


def split(value):
    high = value.astype(jnp.bfloat16)
    low = (value - high.astype(jnp.float32)).astype(jnp.bfloat16)
    return high, low


def dot3(left, right, contract=((1,), (0,))):
    one = functools.partial(lax.dot_general, dimension_numbers=(contract, ((), ())), preferred_element_type=jnp.float32)
    return one(left[0], right[0]) + (one(left[1], right[0]) + one(left[0], right[1]))


def radix4(pieces):
    (ar, ai), (br, bi), (cr, ci), (dr, di) = pieces
    even = (ar + cr, ai + ci)
    odd = (br + dr, bi + di)
    even_less = (ar - cr, ai - ci)
    odd_less = (br - dr, bi - di)
    return [
        (even[0] + odd[0], even[1] + odd[1]),
        (even_less[0] + odd_less[1], even_less[1] - odd_less[0]),
        (even[0] - odd[0], even[1] - odd[1]),
        (even_less[0] - odd_less[1], even_less[1] + odd_less[0]),
    ]


def weights_kernel(starts_ref, ids_ref, table_ref, inverse_ref, out_ref, high_ref, low_ref):
    step = pl.program_id(0)
    block_count, freq_count, _ = table_ref.shape
    tiles = out_ref.shape[0]

    @pl.when(step == 0)
    def _():
        for w in range(block_count):
            for f2 in range(2):
                for fr in range(2):
                    rows = table_ref[w, pl.ds(fr * (freq_count // 2) + f2, freq_count // 4, stride=2), :]
                    high, low = split(rows)
                    at = (f2 * 2 + fr) * (freq_count // 4)
                    high_ref[w, at : at + freq_count // 4, :] = high
                    low_ref[w, at : at + freq_count // 4, :] = low

    for t in range(tiles):
        tile = step * tiles + t
        first, second = ids_ref[2 * tile], ids_ref[2 * tile + 1]
        left = (
            jnp.concatenate([high_ref[first], high_ref[second]], axis=1),
            jnp.concatenate([low_ref[first], low_ref[second]], axis=1),
        )
        rows = pl.ds(pl.multiple_of(starts_ref[tile] * LANES, LANES), 2 * LANES)
        product = dot3(left, (inverse_ref[0, rows, :], inverse_ref[1, rows, :]))
        high, low = split(product)
        for c in range(2):
            at = c * freq_count
            out_ref[t, 0, at : at + freq_count, :] = high[:, c * KZ : (c + 1) * KZ]
            out_ref[t, 1, at : at + freq_count, :] = low[:, c * KZ : (c + 1) * KZ]


def tile_weights(stolt_table, kz_start, weight_ids):
    block_count, freq_count, block_width = stolt_table.shape
    kx_rows, tiles = kz_start.shape
    inverse = inverse_table(KZ)
    return pl.pallas_call(
        weights_kernel,
        grid_spec=pltpu.PrefetchScalarGridSpec(
            num_scalar_prefetch=2,
            grid=(kx_rows,),
            in_specs=[
                pl.BlockSpec(stolt_table.shape, lambda i, *_: (0, 0, 0)),
                pl.BlockSpec(inverse.shape, lambda i, *_: (0, 0, 0)),
            ],
            out_specs=pl.BlockSpec((tiles, 2, 2 * freq_count, KZ), lambda i, *_: (i, 0, 0, 0)),
            scratch_shapes=[pltpu.VMEM(stolt_table.shape, jnp.bfloat16)] * 2,
        ),
        out_shape=jax.ShapeDtypeStruct((kx_rows * tiles, 2, 2 * freq_count, KZ), jnp.bfloat16),
        compiler_params=pltpu.CompilerParams(vmem_limit_bytes=24 << 20),
        name="tile_weights",
    )(kz_start.reshape(-1), weight_ids.reshape(-1), stolt_table, jnp.asarray(inverse))


def forward_x_kernel(x_ref, table_ref, out_ref):
    sources, freqs, _, span, _ = x_ref.shape
    per = sources // 4
    quarter = per * span
    pieces = []
    for q in range(4):
        pieces.append(
            tuple(
                jnp.concatenate([x_ref[q * per : (q + 1) * per, f, c].reshape(quarter, LANES) for f in range(freqs)], axis=1)
                for c in range(2)
            )
        )
    stride = 4 * freqs * 2
    for r, (real, imag) in enumerate(radix4(pieces)):
        right = split(jnp.concatenate([real, imag], axis=0))
        product = dot3((table_ref[r, 0], table_ref[r, 1]), right)
        for c in range(2):
            for f in range(freqs):
                out_ref[pl.ds((r * freqs + f) * 2 + c, quarter, stride=stride), :] = product[
                    c * quarter : (c + 1) * quarter, f * LANES : (f + 1) * LANES
                ]


def forward_x(received):
    sources, freqs, _, span, columns = received.shape
    table = radix4_tables(sources * span)
    return pl.pallas_call(
        forward_x_kernel,
        out_shape=jax.ShapeDtypeStruct((sources * span * freqs * 2, columns), jnp.float32),
        compiler_params=pltpu.CompilerParams(vmem_limit_bytes=40 << 20),
        name="forward_x",
    )(received, jnp.asarray(table))


def image_kernel(s_ref, y_ref, w_ref, out_ref, spec_ref):
    step = pl.program_id(0)
    tiles, _, depth, _ = w_ref.shape
    freq_count = depth // 2
    ky_count = tiles * TK
    kx_rows = spec_ref.shape[1]
    rows_q = s_ref.shape[0] // 4
    message = 4 * kx_rows
    per = freq_count // 4

    @pl.when(step == 0)
    def _():
        halves = [[] for _ in range(4)]
        for r in range(kx_rows):
            pieces = []
            for q in range(4):
                parts = []
                for c in range(2):
                    loaded = [
                        s_ref[pl.ds(q * rows_q + fr * message + (r * 2 + f2) * 2 + c, per, stride=2 * message), :]
                        for f2 in range(2)
                        for fr in range(2)
                    ]
                    parts.append(jnp.concatenate(loaded, axis=0))
                pieces.append(tuple(parts))
            for residue, (real, imag) in enumerate(radix4(pieces)):
                halves[residue].append(split(jnp.concatenate([real, imag], axis=1)))
        for residue in range(4):
            right = tuple(jnp.concatenate([pair[h] for pair in halves[residue]], axis=0) for h in range(2))
            product = dot3((y_ref[residue, 0], y_ref[residue, 1]), right, ((1,), (1,)))
            for c in range(2):
                for r in range(kx_rows):
                    spec_ref[c, r, pl.ds(residue, ky_count // 4, stride=4), :] = product[
                        c * ky_count // 4 : (c + 1) * ky_count // 4, r * freq_count : (r + 1) * freq_count
                    ]

    for t in range(tiles):
        real = split(spec_ref[0, step, t * TK : (t + 1) * TK, :])
        imag = split(spec_ref[1, step, t * TK : (t + 1) * TK, :])
        left = tuple(
            jnp.concatenate(
                [jnp.concatenate([real[h], -imag[h]], axis=1), jnp.concatenate([imag[h], real[h]], axis=1)], axis=0
            )
            for h in range(2)
        )
        product = dot3(left, (w_ref[t, 0], w_ref[t, 1]))
        for c in range(2):
            out_ref[c, 0, t * TK : (t + 1) * TK, :] = product[c * TK : (c + 1) * TK, :]


def form_image(columns, weights, kx_rows):
    tiles = weights.shape[0] // kx_rows
    freq_count = weights.shape[2] // 2
    ky_count = tiles * TK
    table = radix4_tables(ky_count)
    return pl.pallas_call(
        image_kernel,
        grid=(kx_rows,),
        in_specs=[
            pl.BlockSpec(columns.shape, lambda i: (0, 0)),
            pl.BlockSpec(table.shape, lambda i: (0, 0, 0, 0)),
            pl.BlockSpec((tiles,) + weights.shape[1:], lambda i: (i, 0, 0, 0)),
        ],
        out_specs=pl.BlockSpec((2, 1, ky_count, KZ), lambda i: (0, i, 0, 0)),
        scratch_shapes=[pltpu.VMEM((2, kx_rows, ky_count, freq_count), jnp.float32)],
        out_shape=jax.ShapeDtypeStruct((2, kx_rows, ky_count, KZ), jnp.float32),
        compiler_params=pltpu.CompilerParams(vmem_limit_bytes=40 << 20),
        name="form_image",
    )(columns, jnp.asarray(table), weights)


def shards(echoes, stolt_table, kz_start, weight_ids):
    count_ax = lax.axis_size("ax")
    freqs, _, span, columns = echoes.shape
    outgoing = echoes.reshape(count_ax, freqs // count_ax, 2, span, columns)
    received = lax.all_to_all(outgoing, "ax", split_axis=0, concat_axis=0, tiled=True)
    weights = tile_weights(stolt_table, kz_start, weight_ids)
    spectrum = forward_x(received)
    everyone = ("ay", "ax", "fr")
    count = lax.axis_size(everyone)
    messages = spectrum.reshape(count, -1, columns)
    gathered = lax.all_to_all(messages, everyone, split_axis=0, concat_axis=0, tiled=True)
    return form_image(gathered.reshape(-1, columns), weights, kz_start.shape[0])


def solution(mesh):
    placed = (
        P("fr", None, "ax", "ay"),
        P(),
        P(("ay", "ax", "fr"), None),
        P(("ay", "ax", "fr"), None, None),
    )
    return jax.shard_map(
        shards,
        mesh=mesh,
        in_specs=placed,
        out_specs=P(None, ("ay", "ax", "fr"), None, None),
        check_vma=False,
    )
```

profile of v0, /device:TPU:1, one launch (start us, length us, event | category | flops | bytes accessed | tf_op | source)
XLA Modules:
  0.0 140.9 jit_solution(13780055075289994766)
XLA Ops:
  0.0 0.0 copy-start.3
  0.0 60.8 %all_to_all.10.x_ref = f32[32,2,2,32,128]{4,3,2,1,0:T(8,128)S(1)} all-to-all(f32[32,2,2,32,128]{4,3,2,1,0:T(8,128)} %bitcast.5), channel_id=1, replica_groups=mesh['ax'=32,'ay'=4,'fr'=2] {'ax'}, dimensions={0} | all-to-all | bytes 4194304 | tf_op jit(solution)/shard_map/all_to_all | solution.py:230
  60.8 0.0 copy-done.3
  60.8 2.3 %forward_x.1 = f32[4096,128]{1,0:T(8,128)S(1)} custom-call(f32[32,2,2,32,128]{4,3,2,1,0:T(8,128)S(1)} %all_to_all.10.x_ref, bf16[4,2,512,512]{3,2,1,0:T(8,128)(2,1)S(1)} %copy-done.3), custom_call_target="tpu_custom_call" | custom-call | tf_op jit(solution)/shard_map/forward_x/pallas_call | solution.py:147
  63.1 0.0 copy-start.2
  63.1 1.3 copy-done.2
  64.4 0.0 copy-start.8
  64.4 0.0 copy-start.7
  64.4 0.0 copy-start.4
  64.4 10.0 %all-to-all-start.1 = ((f32[256,16,128]{2,1,0:T(8,128)}), f32[256,16,128]{2,1,0:T(8,128)S(1)}, u32[]{:S(2)}, u32[]{:S(2)}) async-start(f32[256,16,128]{2,1,0:T(8,128)} %bitcast.4), calls=%async_computation.1 | async-start | bytes 4194304 | tf_op jit(solution)/shard_map/all_to_all | solution.py:236
  74.4 0.0 copy-done.8
  74.4 0.1 reshape.18.starts_ref
  74.5 0.0 copy-done.7
  74.5 0.1 copy.9
  74.6 0.1 reshape.19.ids_ref
  74.7 0.0 copy-done.4
  74.7 0.0 copy-start.6
  74.7 1.0 copy-done.6
  75.7 3.9 %tile_weights.1.w_ref = bf16[16,2,256,384]{3,2,1,0:T(8,128)(2,1)S(1)} custom-call(s32[16]{0:T(128)S(1)} %reshape.18.starts_ref, s32[32]{0:T(128)S(1)} %reshape.19.ids_ref, f32[8,128,128]{2,1,0:T(8,128)S(1)} %copy-done.6, bf16[2,384,768]{2,1,0:T(8,128)(2,1)S(1)} %copy-done.4), custom_call_target="tpu_custom_call" | custom-call | tf_op jit(solution)/shard_map/tile_weights/pallas_call | solution.py:103
  79.6 0.0 copy-start
  79.6 2.7 %copy-done = bf16[16,2,256,384]{3,2,1,0:T(8,128)(2,1)} copy-done((bf16[16,2,256,384]{3,2,1,0:T(8,128)(2,1)}, bf16[16,2,256,384]{3,2,1,0:T(8,128)(2,1)S(1)}, u32[]{:S(2)}) %copy-start) | copy-done | bytes 6291480
  82.3 46.3 %all-to-all-done.1 = f32[256,16,128]{2,1,0:T(8,128)S(1)} async-done(((f32[256,16,128]{2,1,0:T(8,128)}), f32[256,16,128]{2,1,0:T(8,128)S(1)}, u32[]{:S(2)}, u32[]{:S(2)}) %all-to-all-start.1) | async-done | bytes 2097184 | tf_op jit(solution)/shard_map/all_to_all | solution.py:236
  128.7 0.0 copy-start.1
  128.7 2.8 %copy-done.1 = bf16[16,2,256,384]{3,2,1,0:T(8,128)(2,1)S(1)} copy-done((bf16[16,2,256,384]{3,2,1,0:T(8,128)(2,1)S(1)}, bf16[16,2,256,384]{3,2,1,0:T(8,128)(2,1)}, u32[]{:S(2)}) %copy-start.1) | copy-done | bytes 6291480
  131.5 0.0 copy-start.5
  131.5 1.2 copy-done.5
  132.7 8.2 %form_image.1 = f32[2,4,512,384]{3,2,1,0:T(8,128)} custom-call(f32[4096,128]{1,0:T(8,128)S(1)} %bitcast.3, bf16[4,2,256,256]{3,2,1,0:T(8,128)(2,1)S(1)} %copy-done.5, bf16[16,2,256,384]{3,2,1,0:T(8,128)(2,1)S(1)} %copy-done.1), custom_call_target="tpu_custom_call" | custom-call | tf_op jit(solution)/shard_map/form_image/pallas_call | solution.py:210
Async XLA Ops:
  0.0 60.8 %copy-start.3 = (bf16[4,2,512,512]{3,2,1,0:T(8,128)(2,1)S(1)}, bf16[4,2,512,512]{3,2,1,0:T(8,128)(2,1)}, u32[]{:S(2)}) copy-start(bf16[4,2,512,512]{3,2,1,0:T(8,128)(2,1)} %constant.7.clone.table_ref) | copy-start | bytes 12582916
  63.1 1.3 copy-start.2
  64.4 10.0 %copy-start.8 = (s32[4,4]{1,0:T(4,128)S(1)}, s32[4,4]{1,0:T(4,128)}, u32[]{:S(2)}) copy-start(s32[4,4]{1,0:T(4,128)} %param.9) | copy-start | bytes 196
  64.4 10.1 %copy-start.7 = (s32[4,4,2]{1,2,0:T(2,128)S(1)}, s32[4,4,2]{1,2,0:T(2,128)}, u32[]{:S(2)}) copy-start(s32[4,4,2]{1,2,0:T(2,128)} %param.10) | copy-start | bytes 388
  64.4 10.3 %copy-start.4 = (bf16[2,384,768]{2,1,0:T(8,128)(2,1)S(1)}, bf16[2,384,768]{2,1,0:T(8,128)(2,1)}, u32[]{:S(2)}) copy-start(bf16[2,384,768]{2,1,0:T(8,128)(2,1)} %constant.6.clone.inverse_ref) | copy-start | bytes 3538948
  64.4 64.3 %all-to-all-start.1 = ((f32[256,16,128]{2,1,0:T(8,128)}), f32[256,16,128]{2,1,0:T(8,128)S(1)}, u32[]{:S(2)}, u32[]{:S(2)}) async-start(f32[256,16,128]{2,1,0:T(8,128)} %bitcast.4), calls=%async_computation.1 | async-start | bytes 4194304 | tf_op jit(solution)/shard_map/all_to_all | solution.py:236
  74.7 1.0 copy-start.6
  79.6 2.7 %copy-start = (bf16[16,2,256,384]{3,2,1,0:T(8,128)(2,1)}, bf16[16,2,256,384]{3,2,1,0:T(8,128)(2,1)S(1)}, u32[]{:S(2)}) copy-start(bf16[16,2,256,384]{3,2,1,0:T(8,128)(2,1)S(1)} %tile_weights.1.w_ref) | copy-start | bytes 18874372
  128.7 2.8 %copy-start.1 = (bf16[16,2,256,384]{3,2,1,0:T(8,128)(2,1)S(1)}, bf16[16,2,256,384]{3,2,1,0:T(8,128)(2,1)}, u32[]{:S(2)}) copy-start(bf16[16,2,256,384]{3,2,1,0:T(8,128)(2,1)} %copy-done) | copy-start | bytes 18874372
  131.5 1.2 copy-start.5
where the time goes:
time: 141 us
  blocking collectives  60.8 us (43%)
  waiting for transfers between devices  46.3 us (33%)
  Pallas kernels  14.4 us (10%)
  starting transfers between devices  9.96 us (7%)
  local copies, waits for them, and re-layouts  9.37 us (7%)
    all_to_all x1, blocking collectives, shards(): lax.all_to_all(outgoing, 'ax', split_axis=0, concat_axis=0, tiled=True)  60.8 us
    all_to_all x1, waiting for transfers between devices, shards(): lax.all_to_all(messages, everyone, split_axis=0, concat_axis=0, tiled=True)  46.3 us
    all_to_all x1, starting transfers between devices, shards(): lax.all_to_all(messages, everyone, split_axis=0, concat_axis=0, tiled=True)  9.96 us
    unnamed x19, local copies, waits for them, and re-layouts  9.2 us
    pallas_call x1, Pallas kernels, form_image(): pl.pallas_call(image_kernel, grid=(kx_rows,), in_specs=[pl.BlockSpec(colu...  8.22 us
    pallas_call x1, Pallas kernels, tile_weights(): pl.pallas_call(weights_kernel, grid_spec=pltpu.PrefetchScalarGridSpec(num...  3.88 us
  transfers between devices with their start and end apart: 1, of which 1 were waited for; matrix products, arithmetic and copies ran while one was open for 0% of the time, Pallas kernels for 3%

commit v1 on v0

v1 whole, which is shorter than its diff:
```python
import functools
import math

import jax
import jax.numpy as jnp
import ml_dtypes
import numpy as np
from jax import lax
from jax.experimental import pallas as pl
from jax.experimental.pallas import tpu as pltpu
from jax.sharding import Mesh
from jax.sharding import PartitionSpec as P

TK = 128
KZ = 384
LANES = 128


def halves_of(table):
    high = table.astype(ml_dtypes.bfloat16)
    low = (table - high.astype(np.float64)).astype(ml_dtypes.bfloat16)
    return np.stack([high, low])


def dft_table(length, scale, start=0, step=1, order=None):
    n = np.arange(length // step)
    phase = ((start + step * (n if order is None else order)[:, None]) * n[None, :]) % length
    angle = phase * (2.0 * math.pi / length)
    cosine, sine = np.cos(angle) / scale, np.sin(angle) / scale
    return halves_of(np.block([[cosine, sine], [-sine, cosine]]))


def residue_tables(length):
    return np.stack([dft_table(length, math.sqrt(length), r, 4) for r in range(4)])


def twiddles(length, radix):
    n = np.arange(length // radix)
    table = np.zeros((length // radix, LANES), np.float32)
    for r in range(radix):
        angle = (r * n % length) * (2.0 * math.pi / length)
        table[:, 2 * r], table[:, 2 * r + 1] = np.cos(angle), np.sin(angle)
    return table


def inverse_table(length):
    index = np.arange(length)
    angle = (index[:, None] * index[None, :] % length) * (2.0 * math.pi / length)
    return halves_of(np.concatenate([np.cos(angle), np.sin(angle)], axis=1) / math.sqrt(length))


def split(value):
    high = value.astype(jnp.bfloat16)
    low = (value - high.astype(jnp.float32)).astype(jnp.bfloat16)
    return high, low


def dot3(left, right, contract=((1,), (0,))):
    one = functools.partial(lax.dot_general, dimension_numbers=(contract, ((), ())), preferred_element_type=jnp.float32)
    return one(left[0], right[0]) + (one(left[1], right[0]) + one(left[0], right[1]))


def radix4(pieces):
    (ar, ai), (br, bi), (cr, ci), (dr, di) = pieces
    even = (ar + cr, ai + ci)
    odd = (br + dr, bi + di)
    even_less = (ar - cr, ai - ci)
    odd_less = (br - dr, bi - di)
    return [
        (even[0] + odd[0], even[1] + odd[1]),
        (even_less[0] + odd_less[1], even_less[1] - odd_less[0]),
        (even[0] - odd[0], even[1] - odd[1]),
        (even_less[0] - odd_less[1], even_less[1] + odd_less[0]),
    ]


def radix8(pieces):
    root = math.sqrt(0.5)
    evens, odds = radix4(pieces[0::2]), radix4(pieces[1::2])
    (ar, ai), (br, bi), (cr, ci), (dr, di) = odds
    turned = [(ar, ai), ((br + bi) * root, (bi - br) * root), (ci, -cr), ((di - dr) * root, -(dr + di) * root)]
    return [(e[0] + o[0], e[1] + o[1]) for e, o in zip(evens, turned)] + [
        (e[0] - o[0], e[1] - o[1]) for e, o in zip(evens, turned)
    ]


def weights_kernel(starts_ref, ids_ref, table_ref, inverse_ref, y_ref, out_ref, high_ref, low_ref):
    step = pl.program_id(0)
    block_count, freq_count, _ = table_ref.shape
    tiles = out_ref.shape[0]

    @pl.when(step == 0)
    def _():
        for w in range(block_count):
            high_ref[w], low_ref[w] = split(table_ref[w])

    @pl.when(step < pl.num_programs(0) - 1)
    def _():
        for t in range(tiles):
            tile = step * tiles + t
            first, second = ids_ref[2 * tile], ids_ref[2 * tile + 1]
            left = (
                jnp.concatenate([high_ref[first], high_ref[second]], axis=1),
                jnp.concatenate([low_ref[first], low_ref[second]], axis=1),
            )
            rows = pl.ds(pl.multiple_of(starts_ref[tile] * LANES, LANES), 2 * LANES)
            product = dot3(left, (inverse_ref[0, rows, :], inverse_ref[1, rows, :]))
            high, low = split(product)
            for h, half in enumerate((high, low)):
                for c in range(2):
                    out_ref[t, h, c * freq_count : (c + 1) * freq_count, :] = half[:, c * KZ : (c + 1) * KZ]

    @pl.when(step == pl.num_programs(0) - 1)
    def _():
        width = y_ref.shape[3]
        out_ref[:, :, :, :width] = y_ref[...]
        out_ref[:, :, :, width:] = jnp.zeros_like(out_ref[:, :, :, width:])


def tile_weights(stolt_table, kz_start, weight_ids):
    block_count, freq_count, block_width = stolt_table.shape
    kx_rows, tiles = kz_start.shape
    inverse = inverse_table(KZ)
    residues = residue_tables(tiles * TK)
    return pl.pallas_call(
        weights_kernel,
        grid_spec=pltpu.PrefetchScalarGridSpec(
            num_scalar_prefetch=2,
            grid=(kx_rows + 1,),
            in_specs=[
                pl.BlockSpec(stolt_table.shape, lambda i, *_: (0, 0, 0)),
                pl.BlockSpec(inverse.shape, lambda i, *_: (0, 0, 0)),
                pl.BlockSpec(residues.shape, lambda i, *_: (0, 0, 0, 0)),
            ],
            out_specs=pl.BlockSpec((tiles, 2, 2 * freq_count, KZ), lambda i, *_: (i, 0, 0, 0)),
            scratch_shapes=[pltpu.VMEM(stolt_table.shape, jnp.bfloat16)] * 2,
        ),
        out_shape=jax.ShapeDtypeStruct(((kx_rows + 1) * tiles, 2, 2 * freq_count, KZ), jnp.bfloat16),
        compiler_params=pltpu.CompilerParams(vmem_limit_bytes=24 << 20),
        name="tile_weights",
    )(kz_start.reshape(-1), weight_ids.reshape(-1), stolt_table, jnp.asarray(inverse), jnp.asarray(residues))


def forward_x_kernel(x_ref, twiddle_ref, table_ref, out_ref):
    sources, freqs, _, span, _ = x_ref.shape
    per = sources // 8
    piece = per * span
    pieces = []
    for q in range(8):
        pieces.append(
            tuple(
                jnp.concatenate([x_ref[q * per : (q + 1) * per, f, c].reshape(piece, LANES) for f in range(freqs)], axis=1)
                for c in range(2)
            )
        )
    table = (table_ref[0], table_ref[1])
    message = 4 * freqs * 2
    run = piece // 2
    for r, (real, imag) in enumerate(radix8(pieces)):
        if r > 0:
            cosine, sine = twiddle_ref[:, 2 * r : 2 * r + 1], twiddle_ref[:, 2 * r + 1 : 2 * r + 2]
            real, imag = real * cosine + imag * sine, imag * cosine - real * sine
        product = dot3(table, split(jnp.concatenate([real, imag], axis=0)))
        z_hi, row = r // 4, r % 4
        for c in range(2):
            for core in range(2):
                rows = slice(c * piece + core * run, c * piece + (core + 1) * run)
                for f in range(freqs):
                    at = (core * 2 + z_hi) * run * message + (c * 4 + row) * freqs + f
                    out_ref[pl.ds(at, run, stride=message), :] = product[rows, f * LANES : (f + 1) * LANES]


def forward_x(received, order):
    sources, freqs, _, span, columns = received.shape
    length = sources * span
    twiddle = twiddles(length, 8)
    table = dft_table(length // 8, math.sqrt(length), order=order)
    return pl.pallas_call(
        forward_x_kernel,
        out_shape=jax.ShapeDtypeStruct((length * freqs * 2, columns), jnp.float32),
        compiler_params=pltpu.CompilerParams(vmem_limit_bytes=24 << 20),
        name="forward_x",
    )(received, jnp.asarray(twiddle), jnp.asarray(table))


def image_kernel(s_ref, w_ref, out_ref, spec_ref, stage_ref, out_sems):
    _, kx_rows, ky_count, freq_count = spec_ref.shape
    tiles = ky_count // TK
    message = 4 * kx_rows
    y_tables = w_ref.shape[0] - 4
    y_width = ky_count // 2
    sources = s_ref.shape[0] // (4 * message)
    whole = s_ref[...].reshape(sources, 4, 2, message // 2, LANES)
    turned = [[jnp.swapaxes(whole[:, q, c], 0, 1) for c in range(2)] for q in range(4)]
    for pair in range(0, kx_rows, 2):
        halves = [[] for _ in range(4)]
        for r in range(pair, pair + 2):
            pieces = []
            for q in range(4):
                parts = []
                for c in range(2):
                    rows = turned[q][c]
                    parts.append(jnp.concatenate([rows[r * 2], rows[r * 2 + 1]], axis=0))
                pieces.append(tuple(parts))
            for residue, (real, imag) in enumerate(radix4(pieces)):
                halves[residue].append(split(jnp.concatenate([real, imag], axis=1)))
        for residue in range(4):
            right = tuple(jnp.concatenate([pair_of[h] for pair_of in halves[residue]], axis=0) for h in range(2))
            table = tuple(w_ref[y_tables + residue, h, :, :y_width] for h in range(2))
            product = dot3(table, right, ((1,), (1,)))
            for c in range(2):
                for j in range(2):
                    spec_ref[c, pair + j, pl.ds(residue, ky_count // 4, stride=4), :] = product[
                        c * ky_count // 4 : (c + 1) * ky_count // 4, j * freq_count : (j + 1) * freq_count
                    ]

    copies = []
    for r in range(kx_rows):
        for t in range(tiles):
            rows = slice(t * TK, (t + 1) * TK)
            real = split(spec_ref[0, r, rows, :])
            imag = split(spec_ref[1, r, rows, :])
            left = tuple(jnp.concatenate([real[h], imag[h]], axis=1) for h in range(2))
            tile = r * tiles + t
            right = tuple(
                jnp.concatenate(
                    [
                        jnp.concatenate([w_ref[tile, h, :freq_count], w_ref[tile, h, freq_count:]], axis=1),
                        jnp.concatenate([-w_ref[tile, h, freq_count:], w_ref[tile, h, :freq_count]], axis=1),
                    ],
                    axis=0,
                )
                for h in range(2)
            )
            product = dot3(left, right)
            for c in range(2):
                stage_ref[c, r, rows, :] = product[:, c * KZ : (c + 1) * KZ]
            at = (slice(None), r, pl.ds(t * TK, TK), slice(None))
            copies.append(pltpu.make_async_copy(stage_ref.at[at], out_ref.at[at], out_sems.at[tile]))
            copies[-1].start()
    for copy in copies:
        copy.wait()


def form_image(columns, weights, kx_rows):
    tiles = weights.shape[0] // (kx_rows + 1)
    freq_count = weights.shape[2] // 2
    ky_count = tiles * TK
    shape = (2, kx_rows, ky_count, KZ)
    return pl.pallas_call(
        image_kernel,
        out_specs=pl.BlockSpec(memory_space=pltpu.HBM),
        scratch_shapes=[
            pltpu.VMEM((2, kx_rows, ky_count, freq_count), jnp.float32),
            pltpu.VMEM(shape, jnp.float32),
            pltpu.SemaphoreType.DMA((kx_rows * tiles,)),
        ],
        out_shape=jax.ShapeDtypeStruct(shape, jnp.float32),
        compiler_params=pltpu.CompilerParams(vmem_limit_bytes=28 << 20),
        name="form_image",
    )(columns, weights)


EVERYONE = ("core", "z_hi", "z_lo", "y", "x")


def exchange_order(sizes):
    place = ("x", "y", "z_lo", "core")
    blocks = np.arange(math.prod(sizes[a] for a in place)).reshape([sizes[a] for a in place])
    return blocks.transpose([place.index(a) for a in EVERYONE if a in place]).reshape(-1)


def shards(echoes, stolt_table, kz_start, weight_ids):
    sizes = {a: lax.axis_size(a) for a in EVERYONE}
    ax = ("y", "z_lo", "core")
    count_ax = math.prod(sizes[a] for a in ax)
    freqs, _, span, columns = echoes.shape
    share = freqs // count_ax
    outgoing = echoes.reshape(count_ax, share, 2, span, columns)
    received = lax.all_to_all(outgoing, ax, split_axis=0, concat_axis=0, tiled=True)

    blocks, freq_count, width = stolt_table.shape
    split_table = stolt_table.reshape(blocks, sizes["z_hi"], sizes["y"], sizes["z_lo"], sizes["core"], share, width)
    ordered = split_table.transpose(0, 5, 4, 1, 3, 2, 6).reshape(blocks, freq_count, width)
    weights = tile_weights(ordered, kz_start, weight_ids)

    spectrum = forward_x(received, exchange_order(sizes))
    spectrum, weights = lax.optimization_barrier((spectrum, weights))
    count = math.prod(sizes.values())
    messages = spectrum.reshape(count, -1, columns)
    gathered = lax.all_to_all(messages, EVERYONE, split_axis=0, concat_axis=0, tiled=True)
    return form_image(gathered.reshape(-1, columns), weights, kz_start.shape[0])


def solution(mesh):
    y, z_lo, core = 4, 4, 2
    fine = Mesh(
        mesh.devices.reshape(y, z_lo, core, mesh.shape["ay"], mesh.shape["fr"]), ("y", "z_lo", "core", "x", "z_hi")
    )
    kx = ("x", "y", "z_lo", "core", "z_hi")
    placed = (
        P("z_hi", None, ("y", "z_lo", "core"), "x"),
        P(),
        P(kx, None),
        P(kx, None, None),
    )
    return jax.shard_map(
        shards,
        mesh=fine,
        in_specs=placed,
        out_specs=P(None, kx, None, None),
        check_vma=False,
    )
```

time: 141 us -> 132 us (0.936)
  waiting for transfers between devices: 46.3 us -> 39.8 us
  Pallas kernels: 14.4 us -> 11 us
  blocking collectives: 60.8 us -> 63.8 us
  local copies, waits for them, and re-layouts: 9.37 us -> 6.66 us
    all_to_all x1, waiting for transfers between devices: 46.3 us -> 39.8 us  [shards(): lax.all_to_all(outgoing, ax, split_axis=0, concat_axis=0, tiled=True)]
    unnamed x19 -> x17, local copies, waits for them, and re-layouts: 9.2 us -> 5.23 us
    pallas_call x2, Pallas kernels: 10.5 us -> 6.86 us  [the longest x1 5.14 us: form_image(): pl.pallas_call(image_kernel, out_specs=pl.BlockSpec(memory_space=pltpu.HB...]
    all_to_all x1, blocking collectives: 60.8 us -> 63.8 us  [shards(): lax.all_to_all(messages, EVERYONE, split_axis=0, concat_axis=0, tiled=True)]
  transfers between devices with their start and end apart: 1 -> 1, of which waited for: 1 -> 1; matrix products, arithmetic and copies ran while one was open for 0% -> 1% of each run, Pallas kernels for 3% -> 3%
where the time goes in v1:
time: 132 us
  blocking collectives  63.8 us (48%)
  waiting for transfers between devices  39.8 us (30%)
  Pallas kernels  11 us (8%)
  starting transfers between devices  10.3 us (8%)
  local copies, waits for them, and re-layouts  6.66 us (5%)
    all_to_all x1, blocking collectives, shards(): lax.all_to_all(messages, EVERYONE, split_axis=0, concat_axis=0, tiled=True)  63.8 us
    all_to_all x1, waiting for transfers between devices, shards(): lax.all_to_all(outgoing, ax, split_axis=0, concat_axis=0, tiled=True)  39.8 us
    all_to_all x1, starting transfers between devices, shards(): lax.all_to_all(outgoing, ax, split_axis=0, concat_axis=0, tiled=True)  10.3 us
    unnamed x17, local copies, waits for them, and re-layouts  5.23 us
    pallas_call x1, Pallas kernels, form_image(): pl.pallas_call(image_kernel, out_specs=pl.BlockSpec(memory_space=pltpu.HB...  5.14 us
    pallas_call x1, Pallas kernels, tile_weights(): pl.pallas_call(weights_kernel, grid_spec=pltpu.PrefetchScalarGridSpec(num...  4.09 us
  transfers between devices with their start and end apart: 1, of which 1 were waited for; matrix products, arithmetic and copies ran while one was open for 1% of the time, Pallas kernels for 3%

profile of v1, /device:TPU:1, one launch (start us, length us, event | category | flops | bytes accessed | tf_op | source)
XLA Modules:
  0.0 131.7 jit_solution(932705889404953277)
XLA Ops:
  0.0 0.0 copy-start.7
  0.0 0.0 copy-start.6
  0.0 0.0 copy-start.2
  0.0 10.3 %all-to-all-start = ((f32[32,2,2,32,128]{4,3,2,1,0:T(8,128)}), f32[32,2,2,32,128]{4,3,2,1,0:T(8,128)S(1)}, u32[]{:S(2)}, u32[]{:S(2)}) async-start(f32[32,2,2,32,128]{4,3,2,1,0:T(8,128)} %bitcast.10), calls=%async_computation | async-start | bytes 4194304 | tf_op jit(solution)/shard_map/all_to_all | solution.py:280
  10.4 0.0 copy-done.7
  10.4 0.1 reshape.22.starts_ref
  10.4 0.0 copy-done.6
  10.4 0.1 copy.11
  10.6 0.1 reshape.23.ids_ref
  10.7 1.2 copy.12
  11.9 0.0 copy-done.2
  11.9 0.0 copy-start.3
  11.9 1.2 copy-done.3
  13.1 0.0 copy-start.4
  13.1 4.1 %tile_weights.1.w_ref = bf16[20,2,256,384]{3,2,1,0:T(8,128)(2,1)S(1)} custom-call(s32[16]{0:T(128)S(1)} %reshape.22.starts_ref, s32[32]{0:T(128)S(1)} %reshape.23.ids_ref, f32[8,128,128]{2,1,0:T(8,128)S(1)} %bitcast.9, bf16[2,384,768]{2,1,0:T(8,128)(2,1)S(1)} %copy-done.2, bf16[4,2,256,256]{3,2,1,0:T(8,128)(2,1)S(1)} %copy-done.3), custom_call_target="tpu_custom_call" | custom-call | tf_op jit(solution)/shard_map/tile_weights/pallas_call | solution.py:125
  17.2 0.0 copy-start
  17.3 3.0 %copy-done = bf16[20,2,256,384]{3,2,1,0:T(8,128)(2,1)} copy-done((bf16[20,2,256,384]{3,2,1,0:T(8,128)(2,1)}, bf16[20,2,256,384]{3,2,1,0:T(8,128)(2,1)S(1)}, u32[]{:S(2)}) %copy-start) | copy-done | bytes 7864344
  20.3 39.8 %all-to-all-done.x_ref = f32[32,2,2,32,128]{4,3,2,1,0:T(8,128)S(1)} async-done(((f32[32,2,2,32,128]{4,3,2,1,0:T(8,128)}), f32[32,2,2,32,128]{4,3,2,1,0:T(8,128)S(1)}, u32[]{:S(2)}, u32[]{:S(2)}) %all-to-all-start) | async-done | bytes 2097184 | tf_op jit(solution)/shard_map/all_to_all | solution.py:280
  60.1 0.0 copy-done.4
  60.1 0.0 copy-start.5
  60.1 0.8 copy-done.5
  61.0 0.0 copy-start.1
  61.0 1.7 %forward_x.1 = f32[4096,128]{1,0:T(8,128)S(1)} custom-call(f32[32,2,2,32,128]{4,3,2,1,0:T(8,128)S(1)} %all-to-all-done.x_ref, f32[128,128]{1,0:T(8,128)S(1)} %copy-done.5, bf16[2,256,256]{2,1,0:T(8,128)(2,1)S(1)} %copy-done.4), custom_call_target="tpu_custom_call" | custom-call | tf_op jit(solution)/shard_map/forward_x/pallas_call | solution.py:178
  62.7 63.8 %all_to_all.10 = f32[256,16,128]{2,1,0:T(8,128)S(1)} all-to-all(f32[256,16,128]{2,1,0:T(8,128)S(1)} %bitcast.7), channel_id=1, replica_groups=mesh['y'=4,'z_lo'=4,'core'=2,'x'=4,'z_hi'=2] {'core','z_hi','z_lo','y','x'}, dimensions={0} | all-to-all | bytes 4194304 | tf_op jit(solution)/shard_map/all_to_all | solution.py:291
  126.5 0.0 copy-done.1
  126.5 5.1 %form_image.1 = f32[2,4,512,384]{3,2,1,0:T(8,128)} custom-call(f32[4096,128]{1,0:T(8,128)S(1)} %bitcast.8, bf16[20,2,256,384]{3,2,1,0:T(8,128)(2,1)S(1)} %copy-done.1), custom_call_target="tpu_custom_call" | custom-call | tf_op jit(solution)/shard_map/form_image/pallas_call | solution.py:250
Async XLA Ops:
  0.0 10.4 %copy-start.7 = (s32[4,4]{1,0:T(4,128)S(1)}, s32[4,4]{1,0:T(4,128)}, u32[]{:S(2)}) copy-start(s32[4,4]{1,0:T(4,128)} %param.10) | copy-start | bytes 196
  0.0 10.4 %copy-start.6 = (s32[4,4,2]{1,2,0:T(2,128)S(1)}, s32[4,4,2]{1,2,0:T(2,128)}, u32[]{:S(2)}) copy-start(s32[4,4,2]{1,2,0:T(2,128)} %param.11) | copy-start | bytes 388
  0.0 11.9 %copy-start.2 = (bf16[2,384,768]{2,1,0:T(8,128)(2,1)S(1)}, bf16[2,384,768]{2,1,0:T(8,128)(2,1)}, u32[]{:S(2)}) copy-start(bf16[2,384,768]{2,1,0:T(8,128)(2,1)} %constant.8.clone.inverse_ref) | copy-start | bytes 3538948
  0.0 60.1 %all-to-all-start = ((f32[32,2,2,32,128]{4,3,2,1,0:T(8,128)}), f32[32,2,2,32,128]{4,3,2,1,0:T(8,128)S(1)}, u32[]{:S(2)}, u32[]{:S(2)}) async-start(f32[32,2,2,32,128]{4,3,2,1,0:T(8,128)} %bitcast.10), calls=%async_computation | async-start | bytes 4194304 | tf_op jit(solution)/shard_map/all_to_all | solution.py:280
  11.9 1.2 copy-start.3
  13.1 47.0 %copy-start.4 = (bf16[2,256,256]{2,1,0:T(8,128)(2,1)S(1)}, bf16[2,256,256]{2,1,0:T(8,128)(2,1)}, u32[]{:S(2)}) copy-start(bf16[2,256,256]{2,1,0:T(8,128)(2,1)} %constant.11.clone.table_ref) | copy-start | bytes 786436
  17.2 3.1 %copy-start = (bf16[20,2,256,384]{3,2,1,0:T(8,128)(2,1)}, bf16[20,2,256,384]{3,2,1,0:T(8,128)(2,1)S(1)}, u32[]{:S(2)}) copy-start(bf16[20,2,256,384]{3,2,1,0:T(8,128)(2,1)S(1)} %tile_weights.1.w_ref) | copy-start | bytes 23592964
  60.1 0.8 copy-start.5
  61.0 65.6 %copy-start.1 = (bf16[20,2,256,384]{3,2,1,0:T(8,128)(2,1)S(1)}, bf16[20,2,256,384]{3,2,1,0:T(8,128)(2,1)}, u32[]{:S(2)}) copy-start(bf16[20,2,256,384]{3,2,1,0:T(8,128)(2,1)} %copy-done) | copy-start | bytes 23592964

commit v2 on v1

--- a/solution.py
+++ b/solution.py
@@ -22,9 +22,9 @@
     return np.stack([high, low])
 
 
-def dft_table(length, scale, start=0, step=1, order=None):
+def dft_table(length, scale, start=0, step=1):
     n = np.arange(length // step)
-    phase = ((start + step * (n if order is None else order)[:, None]) * n[None, :]) % length
+    phase = ((start + step * n[:, None]) * n[None, :]) % length
     angle = phase * (2.0 * math.pi / length)
     cosine, sine = np.cos(angle) / scale, np.sin(angle) / scale
     return halves_of(np.block([[cosine, sine], [-sine, cosine]]))
@@ -34,13 +34,24 @@
     return np.stack([dft_table(length, math.sqrt(length), r, 4) for r in range(4)])
 
 
-def twiddles(length, radix):
-    n = np.arange(length // radix)
-    table = np.zeros((length // radix, LANES), np.float32)
-    for r in range(radix):
-        angle = (r * n % length) * (2.0 * math.pi / length)
-        table[:, 2 * r], table[:, 2 * r + 1] = np.cos(angle), np.sin(angle)
-    return table
+def turn(phase, length):
+    shifted = (phase & (length - 1)) + length // 8
+    quadrant = (shifted >> ((length // 4).bit_length() - 1)) & 3
+    angle = ((shifted & (length // 4 - 1)) - length // 8).astype(jnp.float32) * (2.0 * math.pi / length)
+    square = angle * angle
+    sine = 1.0 / 362880
+    for term in (-1.0 / 5040, 1.0 / 120, -1.0 / 6, 1.0):
+        sine = sine * square + term
+    sine = sine * angle
+    cosine = 1.0 / 40320
+    for term in (-1.0 / 720, 1.0 / 24, -0.5, 1.0):
+        cosine = cosine * square + term
+    swapped = (quadrant & 1) == 1
+    first = jnp.where(swapped, sine, cosine)
+    second = jnp.where(swapped, cosine, sine)
+    first = jnp.where(((quadrant + 1) & 2) == 2, -first, first)
+    second = jnp.where((quadrant & 2) == 2, -second, second)
+    return first, second
 
 
 def inverse_table(length):
@@ -141,7 +152,7 @@
     )(kz_start.reshape(-1), weight_ids.reshape(-1), stolt_table, jnp.asarray(inverse), jnp.asarray(residues))
 
 
-def forward_x_kernel(x_ref, twiddle_ref, table_ref, out_ref):
+def forward_x_kernel(order, x_ref, out_ref):
     sources, freqs, _, span, _ = x_ref.shape
     per = sources // 8
     piece = per * span
@@ -153,12 +164,23 @@
                 for c in range(2)
             )
         )
-    table = (table_ref[0], table_ref[1])
+    row = lax.broadcasted_iota(jnp.int32, (piece, piece), 0)
+    n = lax.broadcasted_iota(jnp.int32, (piece, piece), 1)
+    k = sum(((row >> shift) & (size - 1)) * stride for shift, size, stride in order)
+    cosine, sine = turn(k * n, piece)
+    scale = 1.0 / math.sqrt(8 * piece)
+    (cos_high, cos_low), (sin_high, sin_low) = split(cosine * scale), split(sine * scale)
+    table = tuple(
+        jnp.concatenate([jnp.concatenate([c, s], axis=1), jnp.concatenate([-s, c], axis=1)], axis=0)
+        for c, s in ((cos_high, sin_high), (cos_low, sin_low))
+    )
+    column = lax.broadcasted_iota(jnp.int32, (piece, LANES), 1)
+    cosines, sines = turn(lax.broadcasted_iota(jnp.int32, (piece, LANES), 0) * column, 8 * piece)
     message = 4 * freqs * 2
     run = piece // 2
     for r, (real, imag) in enumerate(radix8(pieces)):
         if r > 0:
-            cosine, sine = twiddle_ref[:, 2 * r : 2 * r + 1], twiddle_ref[:, 2 * r + 1 : 2 * r + 2]
+            cosine, sine = cosines[:, r : r + 1], sines[:, r : r + 1]
             real, imag = real * cosine + imag * sine, imag * cosine - real * sine
         product = dot3(table, split(jnp.concatenate([real, imag], axis=0)))
         z_hi, row = r // 4, r % 4
@@ -172,15 +194,12 @@
 
 def forward_x(received, order):
     sources, freqs, _, span, columns = received.shape
-    length = sources * span
-    twiddle = twiddles(length, 8)
-    table = dft_table(length // 8, math.sqrt(length), order=order)
     return pl.pallas_call(
-        forward_x_kernel,
-        out_shape=jax.ShapeDtypeStruct((length * freqs * 2, columns), jnp.float32),
+        functools.partial(forward_x_kernel, order),
+        out_shape=jax.ShapeDtypeStruct((sources * span * freqs * 2, columns), jnp.float32),
         compiler_params=pltpu.CompilerParams(vmem_limit_bytes=24 << 20),
         name="forward_x",
-    )(received, jnp.asarray(twiddle), jnp.asarray(table))
+    )(received)
 
 
 def image_kernel(s_ref, w_ref, out_ref, spec_ref, stage_ref, out_sems):
@@ -265,9 +284,13 @@
 
 
 def exchange_order(sizes):
-    place = ("x", "y", "z_lo", "core")
-    blocks = np.arange(math.prod(sizes[a] for a in place)).reshape([sizes[a] for a in place])
-    return blocks.transpose([place.index(a) for a in EVERYONE if a in place]).reshape(-1)
+    strides, shifts = {}, {}
+    for places, axes in ((strides, ("x", "y", "z_lo", "core")), (shifts, [a for a in EVERYONE if a != "z_hi"])):
+        stride = 1
+        for axis in reversed(axes):
+            places[axis] = stride
+            stride *= sizes[axis]
+    return [(shifts[a].bit_length() - 1, sizes[a], strides[a]) for a in strides]
 
 
 def shards(echoes, stolt_table, kz_start, weight_ids):

time: 132 us -> 131 us (level)
    unnamed x17 -> x13, local copies, waits for them, and re-layouts: 5.23 us -> 4.4 us
where the time goes in v2:
time: 131 us
  blocking collectives  63.8 us (49%)
  waiting for transfers between devices  39.8 us (30%)
  Pallas kernels  11 us (8%)
  starting transfers between devices  10.3 us (8%)
  local copies, waits for them, and re-layouts  5.82 us (4%)
    all_to_all x1, blocking collectives, shards(): lax.all_to_all(messages, EVERYONE, split_axis=0, concat_axis=0, tiled=True)  63.8 us
    all_to_all x1, waiting for transfers between devices, shards(): lax.all_to_all(outgoing, ax, split_axis=0, concat_axis=0, tiled=True)  39.8 us
    all_to_all x1, starting transfers between devices, shards(): lax.all_to_all(outgoing, ax, split_axis=0, concat_axis=0, tiled=True)  10.3 us
    pallas_call x1, Pallas kernels, form_image(): pl.pallas_call(image_kernel, out_specs=pl.BlockSpec(memory_space=pltpu.HB...  5.14 us
    unnamed x13, local copies, waits for them, and re-layouts  4.4 us
    pallas_call x1, Pallas kernels, tile_weights(): pl.pallas_call(weights_kernel, grid_spec=pltpu.PrefetchScalarGridSpec(num...  4.08 us
  transfers between devices with their start and end apart: 1, of which 1 were waited for; matrix products, arithmetic and copies ran while one was open for 1% of the time, Pallas kernels for 3%

profile of v2, /device:TPU:1, one launch (start us, length us, event | category | flops | bytes accessed | tf_op | source)
XLA Modules:
  0.0 130.9 jit_solution(2313278232302739817)
XLA Ops:
  0.0 0.0 copy-start.5
  0.0 0.0 copy-start.4
  0.0 0.0 copy-start.2
  0.0 10.3 %all-to-all-start = ((f32[32,2,2,32,128]{4,3,2,1,0:T(8,128)}), f32[32,2,2,32,128]{4,3,2,1,0:T(8,128)S(1)}, u32[]{:S(2)}, u32[]{:S(2)}) async-start(f32[32,2,2,32,128]{4,3,2,1,0:T(8,128)} %bitcast.10), calls=%async_computation | async-start | bytes 4194304 | tf_op jit(solution)/shard_map/all_to_all | solution.py:303
  10.4 0.0 copy-done.5
  10.4 0.1 reshape.22.starts_ref
  10.4 0.0 copy-done.4
  10.4 0.1 copy.9
  10.6 0.1 reshape.23.ids_ref
  10.7 1.2 copy.10
  11.9 0.0 copy-done.2
  11.9 0.0 copy-start.3
  11.9 1.2 copy-done.3
  13.1 4.1 %tile_weights.1.w_ref = bf16[20,2,256,384]{3,2,1,0:T(8,128)(2,1)S(1)} custom-call(s32[16]{0:T(128)S(1)} %reshape.22.starts_ref, s32[32]{0:T(128)S(1)} %reshape.23.ids_ref, f32[8,128,128]{2,1,0:T(8,128)S(1)} %bitcast.9, bf16[2,384,768]{2,1,0:T(8,128)(2,1)S(1)} %copy-done.2, bf16[4,2,256,256]{3,2,1,0:T(8,128)(2,1)S(1)} %copy-done.3), custom_call_target="tpu_custom_call" | custom-call | tf_op jit(solution)/shard_map/tile_weights/pallas_call | solution.py:136
  17.2 0.0 copy-start
  17.2 3.0 %copy-done = bf16[20,2,256,384]{3,2,1,0:T(8,128)(2,1)} copy-done((bf16[20,2,256,384]{3,2,1,0:T(8,128)(2,1)}, bf16[20,2,256,384]{3,2,1,0:T(8,128)(2,1)S(1)}, u32[]{:S(2)}) %copy-start) | copy-done | bytes 7864344
  20.3 39.8 %all-to-all-done.x_ref = f32[32,2,2,32,128]{4,3,2,1,0:T(8,128)S(1)} async-done(((f32[32,2,2,32,128]{4,3,2,1,0:T(8,128)}), f32[32,2,2,32,128]{4,3,2,1,0:T(8,128)S(1)}, u32[]{:S(2)}, u32[]{:S(2)}) %all-to-all-start) | async-done | bytes 2097184 | tf_op jit(solution)/shard_map/all_to_all | solution.py:303
  60.1 0.0 copy-start.1
  60.1 1.8 %forward_x.1 = f32[4096,128]{1,0:T(8,128)S(1)} custom-call(f32[32,2,2,32,128]{4,3,2,1,0:T(8,128)S(1)} %all-to-all-done.x_ref), custom_call_target="tpu_custom_call" | custom-call | tf_op jit(solution)/shard_map/forward_x/pallas_call | solution.py:197
  61.9 63.8 %all_to_all.10 = f32[256,16,128]{2,1,0:T(8,128)S(1)} all-to-all(f32[256,16,128]{2,1,0:T(8,128)S(1)} %bitcast.7), channel_id=1, replica_groups=mesh['y'=4,'z_lo'=4,'core'=2,'x'=4,'z_hi'=2] {'core','z_hi','z_lo','y','x'}, dimensions={0} | all-to-all | bytes 4194304 | tf_op jit(solution)/shard_map/all_to_all | solution.py:314
  125.7 0.0 copy-done.1
  125.7 5.1 %form_image.1 = f32[2,4,512,384]{3,2,1,0:T(8,128)} custom-call(f32[4096,128]{1,0:T(8,128)S(1)} %bitcast.8, bf16[20,2,256,384]{3,2,1,0:T(8,128)(2,1)S(1)} %copy-done.1), custom_call_target="tpu_custom_call" | custom-call | tf_op jit(solution)/shard_map/form_image/pallas_call | solution.py:269
Async XLA Ops:
  0.0 10.4 %copy-start.5 = (s32[4,4]{1,0:T(4,128)S(1)}, s32[4,4]{1,0:T(4,128)}, u32[]{:S(2)}) copy-start(s32[4,4]{1,0:T(4,128)} %param.8) | copy-start | bytes 196
  0.0 10.4 %copy-start.4 = (s32[4,4,2]{1,2,0:T(2,128)S(1)}, s32[4,4,2]{1,2,0:T(2,128)}, u32[]{:S(2)}) copy-start(s32[4,4,2]{1,2,0:T(2,128)} %param.9) | copy-start | bytes 388
  0.0 11.9 %copy-start.2 = (bf16[2,384,768]{2,1,0:T(8,128)(2,1)S(1)}, bf16[2,384,768]{2,1,0:T(8,128)(2,1)}, u32[]{:S(2)}) copy-start(bf16[2,384,768]{2,1,0:T(8,128)(2,1)} %constant.4.clone.inverse_ref) | copy-start | bytes 3538948
  0.0 60.1 %all-to-all-start = ((f32[32,2,2,32,128]{4,3,2,1,0:T(8,128)}), f32[32,2,2,32,128]{4,3,2,1,0:T(8,128)S(1)}, u32[]{:S(2)}, u32[]{:S(2)}) async-start(f32[32,2,2,32,128]{4,3,2,1,0:T(8,128)} %bitcast.10), calls=%async_computation | async-start | bytes 4194304 | tf_op jit(solution)/shard_map/all_to_all | solution.py:303
  11.9 1.2 copy-start.3
  17.2 3.1 %copy-start = (bf16[20,2,256,384]{3,2,1,0:T(8,128)(2,1)}, bf16[20,2,256,384]{3,2,1,0:T(8,128)(2,1)S(1)}, u32[]{:S(2)}) copy-start(bf16[20,2,256,384]{3,2,1,0:T(8,128)(2,1)S(1)} %tile_weights.1.w_ref) | copy-start | bytes 23592964
  60.1 65.6 %copy-start.1 = (bf16[20,2,256,384]{3,2,1,0:T(8,128)(2,1)S(1)}, bf16[20,2,256,384]{3,2,1,0:T(8,128)(2,1)}, u32[]{:S(2)}) copy-start(bf16[20,2,256,384]{3,2,1,0:T(8,128)(2,1)} %copy-done) | copy-start | bytes 23592964

commit v3 on v2

--- a/solution.py
+++ b/solution.py
@@ -152,7 +152,7 @@
     )(kz_start.reshape(-1), weight_ids.reshape(-1), stolt_table, jnp.asarray(inverse), jnp.asarray(residues))
 
 
-def forward_x_kernel(order, x_ref, out_ref):
+def forward_x_kernel(order, slots, x_ref, out_ref):
     sources, freqs, _, span, _ = x_ref.shape
     per = sources // 8
     piece = per * span
@@ -160,7 +160,10 @@
     for q in range(8):
         pieces.append(
             tuple(
-                jnp.concatenate([x_ref[q * per : (q + 1) * per, f, c].reshape(piece, LANES) for f in range(freqs)], axis=1)
+                jnp.concatenate(
+                    [jnp.concatenate([x_ref[slot, f, c] for slot in slots[q * per : (q + 1) * per]], axis=0) for f in range(freqs)],
+                    axis=1,
+                )
                 for c in range(2)
             )
         )
@@ -177,7 +180,6 @@
     column = lax.broadcasted_iota(jnp.int32, (piece, LANES), 1)
     cosines, sines = turn(lax.broadcasted_iota(jnp.int32, (piece, LANES), 0) * column, 8 * piece)
     message = 4 * freqs * 2
-    run = piece // 2
     for r, (real, imag) in enumerate(radix8(pieces)):
         if r > 0:
             cosine, sine = cosines[:, r : r + 1], sines[:, r : r + 1]
@@ -185,32 +187,34 @@
         product = dot3(table, split(jnp.concatenate([real, imag], axis=0)))
         z_hi, row = r // 4, r % 4
         for c in range(2):
-            for core in range(2):
-                rows = slice(c * piece + core * run, c * piece + (core + 1) * run)
-                for f in range(freqs):
-                    at = (core * 2 + z_hi) * run * message + (c * 4 + row) * freqs + f
-                    out_ref[pl.ds(at, run, stride=message), :] = product[rows, f * LANES : (f + 1) * LANES]
-
-
-def forward_x(received, order):
+            for f in range(freqs):
+                at = z_hi * message + (c * 4 + row) * freqs + f
+                out_ref[pl.ds(at, piece, stride=2 * message), :] = product[
+                    c * piece : (c + 1) * piece, f * LANES : (f + 1) * LANES
+                ]
+
+
+def forward_x(received, order, slots):
     sources, freqs, _, span, columns = received.shape
     return pl.pallas_call(
-        functools.partial(forward_x_kernel, order),
+        functools.partial(forward_x_kernel, order, slots),
         out_shape=jax.ShapeDtypeStruct((sources * span * freqs * 2, columns), jnp.float32),
         compiler_params=pltpu.CompilerParams(vmem_limit_bytes=24 << 20),
         name="forward_x",
     )(received)
 
 
-def image_kernel(s_ref, w_ref, out_ref, spec_ref, stage_ref, out_sems):
+def image_kernel(before, s_ref, w_ref, out_ref, spec_ref, stage_ref, out_sems):
     _, kx_rows, ky_count, freq_count = spec_ref.shape
     tiles = ky_count // TK
     message = 4 * kx_rows
     y_tables = w_ref.shape[0] - 4
     y_width = ky_count // 2
     sources = s_ref.shape[0] // (4 * message)
-    whole = s_ref[...].reshape(sources, 4, 2, message // 2, LANES)
-    turned = [[jnp.swapaxes(whole[:, q, c], 0, 1) for c in range(2)] for q in range(4)]
+    whole = s_ref[...].reshape(before, 4, sources // before, 2, message // 2, LANES)
+    turned = [
+        [jnp.swapaxes(whole[:, q, :, c].reshape(sources, message // 2, LANES), 0, 1) for c in range(2)] for q in range(4)
+    ]
     for pair in range(0, kx_rows, 2):
         halves = [[] for _ in range(4)]
         for r in range(pair, pair + 2):
@@ -261,13 +265,13 @@
         copy.wait()
 
 
-def form_image(columns, weights, kx_rows):
+def form_image(columns, weights, kx_rows, before):
     tiles = weights.shape[0] // (kx_rows + 1)
     freq_count = weights.shape[2] // 2
     ky_count = tiles * TK
     shape = (2, kx_rows, ky_count, KZ)
     return pl.pallas_call(
-        image_kernel,
+        functools.partial(image_kernel, before),
         out_specs=pl.BlockSpec(memory_space=pltpu.HBM),
         scratch_shapes=[
             pltpu.VMEM((2, kx_rows, ky_count, freq_count), jnp.float32),
@@ -280,39 +284,50 @@
     )(columns, weights)
 
 
-EVERYONE = ("core", "z_hi", "z_lo", "y", "x")
-
-
-def exchange_order(sizes):
-    strides, shifts = {}, {}
-    for places, axes in ((strides, ("x", "y", "z_lo", "core")), (shifts, [a for a in EVERYONE if a != "z_hi"])):
-        stride = 1
-        for axis in reversed(axes):
-            places[axis] = stride
-            stride *= sizes[axis]
-    return [(shifts[a].bit_length() - 1, sizes[a], strides[a]) for a in strides]
+APERTURE_X = ("y", "z_lo", "core")
+KX = ("x", "y", "z_lo", "core", "z_hi")
+FIRST = ("y", "core", "z_lo")
+SECOND = ("core", "y", "z_lo", "x", "z_hi")
+
+
+def strides(axes, sizes):
+    result, stride = {}, 1
+    for axis in reversed(axes):
+        result[axis] = stride
+        stride *= sizes[axis]
+    return result
+
+
+def product_of(axes, sizes):
+    return math.prod(sizes[axis] for axis in axes)
 
 
 def shards(echoes, stolt_table, kz_start, weight_ids):
-    sizes = {a: lax.axis_size(a) for a in EVERYONE}
-    ax = ("y", "z_lo", "core")
-    count_ax = math.prod(sizes[a] for a in ax)
+    sizes = {axis: lax.axis_size(axis) for axis in KX}
+    count_ax = product_of(FIRST, sizes)
     freqs, _, span, columns = echoes.shape
     share = freqs // count_ax
     outgoing = echoes.reshape(count_ax, share, 2, span, columns)
-    received = lax.all_to_all(outgoing, ax, split_axis=0, concat_axis=0, tiled=True)
+    received = lax.all_to_all(outgoing, FIRST, split_axis=0, concat_axis=0, tiled=True)
 
     blocks, freq_count, width = stolt_table.shape
-    split_table = stolt_table.reshape(blocks, sizes["z_hi"], sizes["y"], sizes["z_lo"], sizes["core"], share, width)
-    ordered = split_table.transpose(0, 5, 4, 1, 3, 2, 6).reshape(blocks, freq_count, width)
-    weights = tile_weights(ordered, kz_start, weight_ids)
-
-    spectrum = forward_x(received, exchange_order(sizes))
+    held = ("z_hi",) + FIRST
+    arriving = [axis for axis in SECOND if axis != "x"]
+    ordered = stolt_table.reshape((blocks,) + tuple(sizes[axis] for axis in held) + (share, width))
+    ordered = ordered.transpose([0, len(held) + 1] + [1 + held.index(axis) for axis in arriving] + [len(held) + 2])
+    weights = tile_weights(ordered.reshape(blocks, freq_count, width), kz_start, weight_ids)
+
+    in_slot = strides(FIRST, sizes)
+    grid = np.indices([sizes[axis] for axis in APERTURE_X]).reshape(len(APERTURE_X), -1)
+    slots = [int(slot) for slot in sum(grid[i] * in_slot[axis] for i, axis in enumerate(APERTURE_X))]
+    in_row, in_kx = strides(SECOND[:-1], sizes), strides(KX[:-1], sizes)
+    order = [(in_row[axis].bit_length() - 1, sizes[axis], in_kx[axis]) for axis in in_kx]
+    spectrum = forward_x(received, order, slots)
     spectrum, weights = lax.optimization_barrier((spectrum, weights))
-    count = math.prod(sizes.values())
-    messages = spectrum.reshape(count, -1, columns)
-    gathered = lax.all_to_all(messages, EVERYONE, split_axis=0, concat_axis=0, tiled=True)
-    return form_image(gathered.reshape(-1, columns), weights, kz_start.shape[0])
+    messages = spectrum.reshape(product_of(SECOND, sizes), -1, columns)
+    gathered = lax.all_to_all(messages, SECOND, split_axis=0, concat_axis=0, tiled=True)
+    before = product_of(SECOND[: SECOND.index("x")], sizes)
+    return form_image(gathered.reshape(-1, columns), weights, kz_start.shape[0], before)
 
 
 def solution(mesh):
@@ -320,17 +335,16 @@
     fine = Mesh(
         mesh.devices.reshape(y, z_lo, core, mesh.shape["ay"], mesh.shape["fr"]), ("y", "z_lo", "core", "x", "z_hi")
     )
-    kx = ("x", "y", "z_lo", "core", "z_hi")
     placed = (
-        P("z_hi", None, ("y", "z_lo", "core"), "x"),
+        P("z_hi", None, APERTURE_X, "x"),
         P(),
-        P(kx, None),
-        P(kx, None, None),
+        P(KX, None),
+        P(KX, None, None),
     )
     return jax.shard_map(
         shards,
         mesh=fine,
         in_specs=placed,
-        out_specs=P(None, kx, None, None),
+        out_specs=P(None, KX, None, None),
         check_vma=False,
     )

time: 131 us -> 129 us (0.985)
  waiting for transfers between devices: 39.8 us -> 38.1 us
    all_to_all x1, waiting for transfers between devices: 39.8 us -> 38.1 us  [shards(): lax.all_to_all(outgoing, FIRST, split_axis=0, concat_axis=0, tiled=True)]
where the time goes in v3:
time: 129 us
  blocking collectives  63 us (49%)
  waiting for transfers between devices  38.1 us (30%)
  Pallas kernels  11.7 us (9%)
  starting transfers between devices  10.3 us (8%)
  local copies, waits for them, and re-layouts  6.04 us (5%)
    all_to_all x1, blocking collectives, shards(): lax.all_to_all(messages, SECOND, split_axis=0, concat_axis=0, tiled=True)  63 us
    all_to_all x1, waiting for transfers between devices, shards(): lax.all_to_all(outgoing, FIRST, split_axis=0, concat_axis=0, tiled=True)  38.1 us
    all_to_all x1, starting transfers between devices, shards(): lax.all_to_all(outgoing, FIRST, split_axis=0, concat_axis=0, tiled=True)  10.3 us
    pallas_call x1, Pallas kernels, form_image(): pl.pallas_call(functools.partial(image_kernel, before), out_specs=pl.Bloc...  5.07 us
    unnamed x13, local copies, waits for them, and re-layouts  4.4 us
    pallas_call x1, Pallas kernels, tile_weights(): pl.pallas_call(weights_kernel, grid_spec=pltpu.PrefetchScalarGridSpec(num...  4.08 us
  transfers between devices with their start and end apart: 1, of which 1 were waited for; matrix products, arithmetic and copies ran while one was open for 1% of the time, Pallas kernels for 3%

profile of v3, /device:TPU:1, one launch (start us, length us, event | category | flops | bytes accessed | tf_op | source)
XLA Modules:
  0.0 129.2 jit_solution(7316010175710803368)
XLA Ops:
  0.0 0.0 copy-start.5
  0.0 0.0 copy-start.4
  0.0 0.0 copy-start.2
  0.0 10.3 %all-to-all-start = ((f32[32,2,2,32,128]{4,3,2,1,0:T(8,128)}), f32[32,2,2,32,128]{4,3,2,1,0:T(8,128)S(1)}, u32[]{:S(2)}, u32[]{:S(2)}) async-start(f32[32,2,2,32,128]{4,3,2,1,0:T(8,128)} %bitcast.10), calls=%async_computation | async-start | bytes 4194304 | tf_op jit(solution)/shard_map/all_to_all | solution.py:311
  10.4 0.0 copy-done.5
  10.4 0.1 reshape.22.starts_ref
  10.4 0.0 copy-done.4
  10.4 0.1 copy.9
  10.6 0.1 reshape.23.ids_ref
  10.7 1.5 %copy.10 = f32[8,2,4,2,4,2,128]{6,1,4,2,3,5,0:T(2,128)S(1)} copy(f32[8,2,4,2,4,2,128]{6,5,4,3,2,1,0:T(2,128)} %bitcast.11) | data formatting | bytes 1048576 | tf_op jit(solution)/shard_map/reshape | solution.py:316
  12.1 0.0 copy-done.2
  12.1 0.0 copy-start.3
  12.2 1.2 copy-done.3
  13.4 4.1 %tile_weights.1.w_ref = bf16[20,2,256,384]{3,2,1,0:T(8,128)(2,1)S(1)} custom-call(s32[16]{0:T(128)S(1)} %reshape.22.starts_ref, s32[32]{0:T(128)S(1)} %reshape.23.ids_ref, f32[8,128,128]{2,1,0:T(8,128)S(1)} %bitcast.9, bf16[2,384,768]{2,1,0:T(8,128)(2,1)S(1)} %copy-done.2, bf16[4,2,256,256]{3,2,1,0:T(8,128)(2,1)S(1)} %copy-done.3), custom_call_target="tpu_custom_call" | custom-call | tf_op jit(solution)/shard_map/tile_weights/pallas_call | solution.py:136
  17.5 0.0 copy-start
  17.5 3.0 %copy-done = bf16[20,2,256,384]{3,2,1,0:T(8,128)(2,1)} copy-done((bf16[20,2,256,384]{3,2,1,0:T(8,128)(2,1)}, bf16[20,2,256,384]{3,2,1,0:T(8,128)(2,1)S(1)}, u32[]{:S(2)}) %copy-start) | copy-done | bytes 7864344
  20.5 38.1 %all-to-all-done.x_ref = f32[32,2,2,32,128]{4,3,2,1,0:T(8,128)S(1)} async-done(((f32[32,2,2,32,128]{4,3,2,1,0:T(8,128)}), f32[32,2,2,32,128]{4,3,2,1,0:T(8,128)S(1)}, u32[]{:S(2)}, u32[]{:S(2)}) %all-to-all-start) | async-done | bytes 2097184 | tf_op jit(solution)/shard_map/all_to_all | solution.py:311
  58.6 0.0 copy-start.1
  58.6 2.5 %forward_x.1 = f32[4096,128]{1,0:T(8,128)S(1)} custom-call(f32[32,2,2,32,128]{4,3,2,1,0:T(8,128)S(1)} %all-to-all-done.x_ref), custom_call_target="tpu_custom_call" | custom-call | tf_op jit(solution)/shard_map/forward_x/pallas_call | solution.py:199
  61.1 63.0 %all_to_all.10 = f32[256,16,128]{2,1,0:T(8,128)S(1)} all-to-all(f32[256,16,128]{2,1,0:T(8,128)S(1)} %bitcast.7), channel_id=1, replica_groups=mesh['y'=4,'z_lo'=4,'core'=2,'x'=4,'z_hi'=2] {'core','y','z_lo','x','z_hi'}, dimensions={0} | all-to-all | bytes 4194304 | tf_op jit(solution)/shard_map/all_to_all | solution.py:328
  124.1 0.0 copy-done.1
  124.1 5.1 %form_image.1 = f32[2,4,512,384]{3,2,1,0:T(8,128)} custom-call(f32[4096,128]{1,0:T(8,128)S(1)} %bitcast.8, bf16[20,2,256,384]{3,2,1,0:T(8,128)(2,1)S(1)} %copy-done.1), custom_call_target="tpu_custom_call" | custom-call | tf_op jit(solution)/shard_map/form_image/pallas_call | solution.py:273
Async XLA Ops:
  0.0 10.4 %copy-start.5 = (s32[4,4]{1,0:T(4,128)S(1)}, s32[4,4]{1,0:T(4,128)}, u32[]{:S(2)}) copy-start(s32[4,4]{1,0:T(4,128)} %param.8) | copy-start | bytes 196
  0.0 10.4 %copy-start.4 = (s32[4,4,2]{1,2,0:T(2,128)S(1)}, s32[4,4,2]{1,2,0:T(2,128)}, u32[]{:S(2)}) copy-start(s32[4,4,2]{1,2,0:T(2,128)} %param.9) | copy-start | bytes 388
  0.0 12.1 %copy-start.2 = (bf16[2,384,768]{2,1,0:T(8,128)(2,1)S(1)}, bf16[2,384,768]{2,1,0:T(8,128)(2,1)}, u32[]{:S(2)}) copy-start(bf16[2,384,768]{2,1,0:T(8,128)(2,1)} %constant.4.clone.inverse_ref) | copy-start | bytes 3538948
  0.0 58.6 %all-to-all-start = ((f32[32,2,2,32,128]{4,3,2,1,0:T(8,128)}), f32[32,2,2,32,128]{4,3,2,1,0:T(8,128)S(1)}, u32[]{:S(2)}, u32[]{:S(2)}) async-start(f32[32,2,2,32,128]{4,3,2,1,0:T(8,128)} %bitcast.10), calls=%async_computation | async-start | bytes 4194304 | tf_op jit(solution)/shard_map/all_to_all | solution.py:311
  12.1 1.2 copy-start.3
  17.5 3.1 %copy-start = (bf16[20,2,256,384]{3,2,1,0:T(8,128)(2,1)}, bf16[20,2,256,384]{3,2,1,0:T(8,128)(2,1)S(1)}, u32[]{:S(2)}) copy-start(bf16[20,2,256,384]{3,2,1,0:T(8,128)(2,1)S(1)} %tile_weights.1.w_ref) | copy-start | bytes 23592964
  58.6 65.5 %copy-start.1 = (bf16[20,2,256,384]{3,2,1,0:T(8,128)(2,1)S(1)}, bf16[20,2,256,384]{3,2,1,0:T(8,128)(2,1)}, u32[]{:S(2)}) copy-start(bf16[20,2,256,384]{3,2,1,0:T(8,128)(2,1)} %copy-done) | copy-start | bytes 23592964

commit v4 on v3

--- a/solution.py
+++ b/solution.py
@@ -179,26 +179,26 @@
     )
     column = lax.broadcasted_iota(jnp.int32, (piece, LANES), 1)
     cosines, sines = turn(lax.broadcasted_iota(jnp.int32, (piece, LANES), 0) * column, 8 * piece)
-    message = 4 * freqs * 2
+    lines = []
     for r, (real, imag) in enumerate(radix8(pieces)):
         if r > 0:
             cosine, sine = cosines[:, r : r + 1], sines[:, r : r + 1]
             real, imag = real * cosine + imag * sine, imag * cosine - real * sine
         product = dot3(table, split(jnp.concatenate([real, imag], axis=0)))
-        z_hi, row = r // 4, r % 4
-        for c in range(2):
-            for f in range(freqs):
-                at = z_hi * message + (c * 4 + row) * freqs + f
-                out_ref[pl.ds(at, piece, stride=2 * message), :] = product[
-                    c * piece : (c + 1) * piece, f * LANES : (f + 1) * LANES
-                ]
+        lines += [
+            product[c * piece : (c + 1) * piece, f * LANES : (f + 1) * LANES] for c in range(2) for f in range(freqs)
+        ]
+        if r % 4 == 3:
+            order_out = [(row * 2 + c) * freqs + f for c in range(2) for row in range(4) for f in range(freqs)]
+            out_ref[:, r // 4] = jnp.swapaxes(jnp.stack([lines[line] for line in order_out]), 0, 1)
+            lines = []
 
 
 def forward_x(received, order, slots):
     sources, freqs, _, span, columns = received.shape
     return pl.pallas_call(
         functools.partial(forward_x_kernel, order, slots),
-        out_shape=jax.ShapeDtypeStruct((sources * span * freqs * 2, columns), jnp.float32),
+        out_shape=jax.ShapeDtypeStruct((sources * span // 8, 2, 8 * freqs, columns), jnp.float32),
         compiler_params=pltpu.CompilerParams(vmem_limit_bytes=24 << 20),
         name="forward_x",
     )(received)

time: 129 us -> 129 us (level)
  no operation moved by 1% of the time
where the time goes in v4:
time: 129 us; the launch traced here: 128 us
  blocking collectives  63 us (49%)
  waiting for transfers between devices  38.1 us (30%)
  Pallas kernels  10.9 us (8%)
  starting transfers between devices  10.3 us (8%)
  local copies, waits for them, and re-layouts  6.04 us (5%)
    all_to_all x1, blocking collectives, shards(): lax.all_to_all(messages, SECOND, split_axis=0, concat_axis=0, tiled=True)  63 us
    all_to_all x1, waiting for transfers between devices, shards(): lax.all_to_all(outgoing, FIRST, split_axis=0, concat_axis=0, tiled=True)  38.1 us
    all_to_all x1, starting transfers between devices, shards(): lax.all_to_all(outgoing, FIRST, split_axis=0, concat_axis=0, tiled=True)  10.3 us
    pallas_call x1, Pallas kernels, form_image(): pl.pallas_call(functools.partial(image_kernel, before), out_specs=pl.Bloc...  5.07 us
    unnamed x13, local copies, waits for them, and re-layouts  4.4 us
    pallas_call x1, Pallas kernels, tile_weights(): pl.pallas_call(weights_kernel, grid_spec=pltpu.PrefetchScalarGridSpec(num...  4.08 us
  transfers between devices with their start and end apart: 1, of which 1 were waited for; matrix products, arithmetic and copies ran while one was open for 1% of the time, Pallas kernels for 3%

profile of v4, /device:TPU:1, one launch (start us, length us, event | category | flops | bytes accessed | tf_op | source)
XLA Modules:
  0.0 128.5 jit_solution(10737513608758894635)
XLA Ops:
  0.0 0.0 copy-start.5
  0.0 0.0 copy-start.4
  0.0 0.0 copy-start.2
  0.0 10.3 %all-to-all-start = ((f32[32,2,2,32,128]{4,3,2,1,0:T(8,128)}), f32[32,2,2,32,128]{4,3,2,1,0:T(8,128)S(1)}, u32[]{:S(2)}, u32[]{:S(2)}) async-start(f32[32,2,2,32,128]{4,3,2,1,0:T(8,128)} %bitcast.10), calls=%async_computation | async-start | bytes 4194304 | tf_op jit(solution)/shard_map/all_to_all | solution.py:311
  10.4 0.0 copy-done.5
  10.4 0.1 reshape.22.starts_ref
  10.4 0.0 copy-done.4
  10.4 0.1 copy.9
  10.6 0.1 reshape.23.ids_ref
  10.7 1.5 %copy.10 = f32[8,2,4,2,4,2,128]{6,1,4,2,3,5,0:T(2,128)S(1)} copy(f32[8,2,4,2,4,2,128]{6,5,4,3,2,1,0:T(2,128)} %bitcast.11) | data formatting | bytes 1048576 | tf_op jit(solution)/shard_map/reshape | solution.py:316
  12.1 0.0 copy-done.2
  12.1 0.0 copy-start.3
  12.2 1.2 copy-done.3
  13.4 4.1 %tile_weights.1.w_ref = bf16[20,2,256,384]{3,2,1,0:T(8,128)(2,1)S(1)} custom-call(s32[16]{0:T(128)S(1)} %reshape.22.starts_ref, s32[32]{0:T(128)S(1)} %reshape.23.ids_ref, f32[8,128,128]{2,1,0:T(8,128)S(1)} %bitcast.9, bf16[2,384,768]{2,1,0:T(8,128)(2,1)S(1)} %copy-done.2, bf16[4,2,256,256]{3,2,1,0:T(8,128)(2,1)S(1)} %copy-done.3), custom_call_target="tpu_custom_call" | custom-call | tf_op jit(solution)/shard_map/tile_weights/pallas_call | solution.py:136
  17.5 0.0 copy-start
  17.5 3.0 %copy-done = bf16[20,2,256,384]{3,2,1,0:T(8,128)(2,1)} copy-done((bf16[20,2,256,384]{3,2,1,0:T(8,128)(2,1)}, bf16[20,2,256,384]{3,2,1,0:T(8,128)(2,1)S(1)}, u32[]{:S(2)}) %copy-start) | copy-done | bytes 7864344
  20.5 38.1 %all-to-all-done.x_ref = f32[32,2,2,32,128]{4,3,2,1,0:T(8,128)S(1)} async-done(((f32[32,2,2,32,128]{4,3,2,1,0:T(8,128)}), f32[32,2,2,32,128]{4,3,2,1,0:T(8,128)S(1)}, u32[]{:S(2)}, u32[]{:S(2)}) %all-to-all-start) | async-done | bytes 2097184 | tf_op jit(solution)/shard_map/all_to_all | solution.py:311
  58.6 0.0 copy-start.1
  58.6 1.8 %forward_x.1 = f32[128,2,16,128]{3,2,1,0:T(8,128)S(1)} custom-call(f32[32,2,2,32,128]{4,3,2,1,0:T(8,128)S(1)} %all-to-all-done.x_ref), custom_call_target="tpu_custom_call" | custom-call | tf_op jit(solution)/shard_map/forward_x/pallas_call | solution.py:199
  60.4 63.0 %all_to_all.10 = f32[256,16,128]{2,1,0:T(8,128)S(1)} all-to-all(f32[256,16,128]{2,1,0:T(8,128)S(1)} %bitcast.7), channel_id=1, replica_groups=mesh['y'=4,'z_lo'=4,'core'=2,'x'=4,'z_hi'=2] {'core','y','z_lo','x','z_hi'}, dimensions={0} | all-to-all | bytes 4194304 | tf_op jit(solution)/shard_map/all_to_all | solution.py:328
  123.4 0.0 copy-done.1
  123.4 5.1 %form_image.1 = f32[2,4,512,384]{3,2,1,0:T(8,128)} custom-call(f32[4096,128]{1,0:T(8,128)S(1)} %bitcast.8, bf16[20,2,256,384]{3,2,1,0:T(8,128)(2,1)S(1)} %copy-done.1), custom_call_target="tpu_custom_call" | custom-call | tf_op jit(solution)/shard_map/form_image/pallas_call | solution.py:273
Async XLA Ops:
  0.0 10.4 %copy-start.5 = (s32[4,4]{1,0:T(4,128)S(1)}, s32[4,4]{1,0:T(4,128)}, u32[]{:S(2)}) copy-start(s32[4,4]{1,0:T(4,128)} %param.8) | copy-start | bytes 196
  0.0 10.4 %copy-start.4 = (s32[4,4,2]{1,2,0:T(2,128)S(1)}, s32[4,4,2]{1,2,0:T(2,128)}, u32[]{:S(2)}) copy-start(s32[4,4,2]{1,2,0:T(2,128)} %param.9) | copy-start | bytes 388
  0.0 12.1 %copy-start.2 = (bf16[2,384,768]{2,1,0:T(8,128)(2,1)S(1)}, bf16[2,384,768]{2,1,0:T(8,128)(2,1)}, u32[]{:S(2)}) copy-start(bf16[2,384,768]{2,1,0:T(8,128)(2,1)} %constant.4.clone.inverse_ref) | copy-start | bytes 3538948
  0.0 58.6 %all-to-all-start = ((f32[32,2,2,32,128]{4,3,2,1,0:T(8,128)}), f32[32,2,2,32,128]{4,3,2,1,0:T(8,128)S(1)}, u32[]{:S(2)}, u32[]{:S(2)}) async-start(f32[32,2,2,32,128]{4,3,2,1,0:T(8,128)} %bitcast.10), calls=%async_computation | async-start | bytes 4194304 | tf_op jit(solution)/shard_map/all_to_all | solution.py:311
  12.1 1.2 copy-start.3
  17.5 3.1 %copy-start = (bf16[20,2,256,384]{3,2,1,0:T(8,128)(2,1)}, bf16[20,2,256,384]{3,2,1,0:T(8,128)(2,1)S(1)}, u32[]{:S(2)}) copy-start(bf16[20,2,256,384]{3,2,1,0:T(8,128)(2,1)S(1)} %tile_weights.1.w_ref) | copy-start | bytes 23592964
  58.6 64.8 %copy-start.1 = (bf16[20,2,256,384]{3,2,1,0:T(8,128)(2,1)S(1)}, bf16[20,2,256,384]{3,2,1,0:T(8,128)(2,1)}, u32[]{:S(2)}) copy-start(bf16[20,2,256,384]{3,2,1,0:T(8,128)(2,1)} %copy-done) | copy-start | bytes 23592964

commit v5 on v4

--- a/solution.py
+++ b/solution.py
@@ -199,7 +199,7 @@
     return pl.pallas_call(
         functools.partial(forward_x_kernel, order, slots),
         out_shape=jax.ShapeDtypeStruct((sources * span // 8, 2, 8 * freqs, columns), jnp.float32),
-        compiler_params=pltpu.CompilerParams(vmem_limit_bytes=24 << 20),
+        compiler_params=pltpu.CompilerParams(vmem_limit_bytes=50 << 20),
         name="forward_x",
     )(received)
 

time: 129 us -> 131 us (1.016)
  waiting for transfers between devices: 38.1 us -> 40.4 us
  local copies, waits for them, and re-layouts: 6.04 us -> 3.78 us
  Pallas kernels: 10.9 us -> 12.7 us
    all_to_all x1, waiting for transfers between devices: 38.1 us -> 40.4 us  [shards(): lax.all_to_all(outgoing, FIRST, split_axis=0, concat_axis=0, tiled=True)]
    pallas_call x1, Pallas kernels: 1.78 us -> 3.56 us  [forward_x(): pl.pallas_call(functools.partial(forward_x_kernel, order, slots), out_sha...]
    unnamed x13 -> x15, local copies, waits for them, and re-layouts: 4.4 us -> 3.18 us
where the time goes in v5:
time: 131 us
  blocking collectives  63 us (48%)
  waiting for transfers between devices  40.4 us (31%)
  Pallas kernels  12.7 us (10%)
  starting transfers between devices  10.5 us (8%)
  local copies, waits for them, and re-layouts  3.78 us (3%)
    all_to_all x1, blocking collectives, shards(): lax.all_to_all(messages, SECOND, split_axis=0, concat_axis=0, tiled=True)  63 us
    all_to_all x1, waiting for transfers between devices, shards(): lax.all_to_all(outgoing, FIRST, split_axis=0, concat_axis=0, tiled=True)  40.4 us
    all_to_all x1, starting transfers between devices, shards(): lax.all_to_all(outgoing, FIRST, split_axis=0, concat_axis=0, tiled=True)  10.5 us
    pallas_call x1, Pallas kernels, form_image(): pl.pallas_call(functools.partial(image_kernel, before), out_specs=pl.Bloc...  5.07 us
    pallas_call x1, Pallas kernels, tile_weights(): pl.pallas_call(weights_kernel, grid_spec=pltpu.PrefetchScalarGridSpec(num...  4.09 us
    pallas_call x1, Pallas kernels, forward_x(): pl.pallas_call(functools.partial(forward_x_kernel, order, slots), out_sha...  3.56 us
    unnamed x15, local copies, waits for them, and re-layouts  3.18 us
  transfers between devices with their start and end apart: 1, of which 1 were waited for; matrix products, arithmetic and copies ran while one was open for 1% of the time, Pallas kernels for 3%

profile of v5, /device:TPU:1, one launch (start us, length us, event | category | flops | bytes accessed | tf_op | source)
XLA Modules:
  0.0 130.5 jit_solution(4574818537530739180)
XLA Ops:
  0.0 0.0 copy-start.6
  0.0 0.0 copy-start.5
  0.0 0.0 copy-start.4
  0.0 0.0 copy-start.2
  0.0 0.0 copy-start.3
  0.0 10.5 %all-to-all-start = ((f32[32,2,2,32,128]{4,3,2,1,0:T(8,128)}), f32[32,2,2,32,128]{4,3,2,1,0:T(8,128)}, u32[]{:S(2)}, u32[]{:S(2)}) async-start(f32[32,2,2,32,128]{4,3,2,1,0:T(8,128)} %bitcast.10), calls=%async_computation | async-start | bytes 4194304 | tf_op jit(solution)/shard_map/all_to_all | solution.py:311
  10.6 0.0 copy-done.6
  10.6 0.1 reshape.22.starts_ref
  10.7 0.0 copy-done.5
  10.7 0.1 copy.9
  10.8 0.1 reshape.23.ids_ref
  10.9 0.0 copy-done.4
  10.9 0.4 copy.10
  11.3 0.0 copy-done.2
  11.3 0.0 copy-done.3
  11.3 4.1 %tile_weights.1.w_ref = bf16[20,2,256,384]{3,2,1,0:T(8,128)(2,1)S(1)} custom-call(s32[16]{0:T(128)S(1)} %reshape.22.starts_ref, s32[32]{0:T(128)S(1)} %reshape.23.ids_ref, f32[8,128,128]{2,1,0:T(8,128)S(1)} %bitcast.9, bf16[2,384,768]{2,1,0:T(8,128)(2,1)S(1)} %copy-done.2, bf16[4,2,256,256]{3,2,1,0:T(8,128)(2,1)S(1)} %copy-done.3), custom_call_target="tpu_custom_call" | custom-call | tf_op jit(solution)/shard_map/tile_weights/pallas_call | solution.py:136
  15.4 0.0 copy-start
  15.4 3.0 %copy-done = bf16[20,2,256,384]{3,2,1,0:T(8,128)(2,1)} copy-done((bf16[20,2,256,384]{3,2,1,0:T(8,128)(2,1)}, bf16[20,2,256,384]{3,2,1,0:T(8,128)(2,1)S(1)}, u32[]{:S(2)}) %copy-start) | copy-done | bytes 7864344
  18.5 40.4 %all-to-all-done.x_ref = f32[32,2,2,32,128]{4,3,2,1,0:T(8,128)} async-done(((f32[32,2,2,32,128]{4,3,2,1,0:T(8,128)}), f32[32,2,2,32,128]{4,3,2,1,0:T(8,128)}, u32[]{:S(2)}, u32[]{:S(2)}) %all-to-all-start) | async-done | bytes 2097184 | tf_op jit(solution)/shard_map/all_to_all | solution.py:311
  58.9 0.0 copy-start.1
  58.9 3.6 %forward_x.1 = f32[128,2,16,128]{3,2,1,0:T(8,128)S(1)} custom-call(f32[32,2,2,32,128]{4,3,2,1,0:T(8,128)} %all-to-all-done.x_ref), custom_call_target="tpu_custom_call" | custom-call | tf_op jit(solution)/shard_map/forward_x/pallas_call | solution.py:199
  62.4 63.0 %all_to_all.10 = f32[256,16,128]{2,1,0:T(8,128)S(1)} all-to-all(f32[256,16,128]{2,1,0:T(8,128)S(1)} %bitcast.7), channel_id=1, replica_groups=mesh['y'=4,'z_lo'=4,'core'=2,'x'=4,'z_hi'=2] {'core','y','z_lo','x','z_hi'}, dimensions={0} | all-to-all | bytes 4194304 | tf_op jit(solution)/shard_map/all_to_all | solution.py:328
  125.4 0.0 copy-done.1
  125.4 5.1 %form_image.1 = f32[2,4,512,384]{3,2,1,0:T(8,128)} custom-call(f32[4096,128]{1,0:T(8,128)S(1)} %bitcast.8, bf16[20,2,256,384]{3,2,1,0:T(8,128)(2,1)S(1)} %copy-done.1), custom_call_target="tpu_custom_call" | custom-call | tf_op jit(solution)/shard_map/form_image/pallas_call | solution.py:273
Async XLA Ops:
  0.0 10.6 %copy-start.6 = (s32[4,4]{1,0:T(4,128)S(1)}, s32[4,4]{1,0:T(4,128)}, u32[]{:S(2)}) copy-start(s32[4,4]{1,0:T(4,128)} %param.8) | copy-start | bytes 196
  0.0 10.7 %copy-start.5 = (s32[4,4,2]{1,2,0:T(2,128)S(1)}, s32[4,4,2]{1,2,0:T(2,128)}, u32[]{:S(2)}) copy-start(s32[4,4,2]{1,2,0:T(2,128)} %param.9) | copy-start | bytes 388
  0.0 10.9 %copy-start.4 = (f32[8,128,128]{2,1,0:T(8,128)S(1)}, f32[8,128,128]{2,1,0:T(8,128)}, u32[]{:S(2)}) copy-start(f32[8,128,128]{2,1,0:T(8,128)} %param.7) | copy-start | bytes 1572868
  0.0 11.3 %copy-start.2 = (bf16[2,384,768]{2,1,0:T(8,128)(2,1)S(1)}, bf16[2,384,768]{2,1,0:T(8,128)(2,1)}, u32[]{:S(2)}) copy-start(bf16[2,384,768]{2,1,0:T(8,128)(2,1)} %constant.4.clone.inverse_ref) | copy-start | bytes 3538948
  0.0 11.3 %copy-start.3 = (bf16[4,2,256,256]{3,2,1,0:T(8,128)(2,1)S(1)}, bf16[4,2,256,256]{3,2,1,0:T(8,128)(2,1)}, u32[]{:S(2)}) copy-start(bf16[4,2,256,256]{3,2,1,0:T(8,128)(2,1)} %constant.5.clone.y_ref) | copy-start | bytes 3145732
  0.0 58.8 %all-to-all-start = ((f32[32,2,2,32,128]{4,3,2,1,0:T(8,128)}), f32[32,2,2,32,128]{4,3,2,1,0:T(8,128)}, u32[]{:S(2)}, u32[]{:S(2)}) async-start(f32[32,2,2,32,128]{4,3,2,1,0:T(8,128)} %bitcast.10), calls=%async_computation | async-start | bytes 4194304 | tf_op jit(solution)/shard_map/all_to_all | solution.py:311
  15.4 3.1 %copy-start = (bf16[20,2,256,384]{3,2,1,0:T(8,128)(2,1)}, bf16[20,2,256,384]{3,2,1,0:T(8,128)(2,1)S(1)}, u32[]{:S(2)}) copy-start(bf16[20,2,256,384]{3,2,1,0:T(8,128)(2,1)S(1)} %tile_weights.1.w_ref) | copy-start | bytes 23592964
  58.9 66.6 %copy-start.1 = (bf16[20,2,256,384]{3,2,1,0:T(8,128)(2,1)S(1)}, bf16[20,2,256,384]{3,2,1,0:T(8,128)(2,1)}, u32[]{:S(2)}) copy-start(bf16[20,2,256,384]{3,2,1,0:T(8,128)(2,1)} %copy-done) | copy-start | bytes 23592964
